TPU v7x, 128 devices: a whole 4x4x4 slice. The times are simulated.
128 devices in a mesh: ctx: 8 (over y, x_lo), fsdp: 16 (over x_hi, z, core).
Axes of the slice: x: 4 (x_hi: 2, x_lo: 2; x = x_hi * 2 + x_lo), y: 4, z: 4, core: 2. Of those that a mesh axis runs over, the one named last changes fastest.
Arguments:
- hidden_in: bfloat16 [16, 1024, 1536], P('fsdp', 'ctx'), may hold values from -6 to 6
- block_order: int32 [16, 16], P('fsdp'), may hold values from 0 to 15, as said below
- attn_gain: bfloat16 [1536], P('fsdp'), may hold values from 0.099609375 to 1.8984375
- w_qkv: bfloat16 [1536, 2048], P('fsdp'), may hold values from -0.21875 to 0.21875
- b_qkv: bfloat16 [2048], P('fsdp'), may hold values from -3 to 3
- w_out: bfloat16 [1536, 1536], P('fsdp'), may hold values from -0.625 to 0.625
- mlp_gain: bfloat16 [1536], P('fsdp'), may hold values from 0.099609375 to 1.8984375
- w_gate_up: bfloat16 [1536, 17920], P('fsdp'), may hold values from -0.15625 to 0.15625
- w_down: bfloat16 [8960, 1536], P('fsdp'), may hold values from -0.09375 to 0.09375
- cotangent: bfloat16 [16, 1024, 1536], P('fsdp', 'ctx'), may hold values from -6 to 6
Outputs:
- hidden_out: float32 [16, 1024, 1536], P('fsdp', 'ctx')
- grad_in: float32 [16, 1024, 1536], P('fsdp', 'ctx')
- grad_attn_gain: float32 [1536], P('fsdp')
- grad_w_qkv: float32 [1536, 2048], P('fsdp')
- grad_b_qkv: float32 [2048], P('fsdp')
- grad_w_out: float32 [1536, 1536], P('fsdp')
- grad_mlp_gain: float32 [1536], P('fsdp')
- grad_w_gate_up: float32 [1536, 17920], P('fsdp')
- grad_w_down: float32 [8960, 1536], P('fsdp')
Inputs may be any that keep to these rules, and one draw needn't show every extreme that they name: `block_order`: each row holds every number 0 to 15 once, and columns 2 c and 2 c + 1 hold two numbers that add up to 15.
All inputs are finite; a program needn't handle non-finite values.
Results may differ from a plain program's by a relative error of at most 0.025.
Values may be sent and summed in bfloat16 or wider, within the bound.
No kernel may reach another device: no remote copies, remote signals or barrier semaphores. Data moves between devices by JAX's collectives and lax.ppermute only.
A program may use at most 448 MiB of HBM per device.

v0:
```python
import math

import jax
import jax.numpy as jnp
from jax import lax
from jax.sharding import PartitionSpec as P

D = 1536
H = 12
KVH = 2
HD = 128
FF = 8960


eps = 1e-06
rope_base = 1000000.0
masked_value = -1e30


def passed_along(block, axis, distance):
    devices = range(lax.axis_size(axis))
    route = [((i - distance) % len(devices), i) for i in devices]
    return lax.ppermute(block, axis, route)


def as_sent(x):

    def short(part):
        return part.astype(jnp.bfloat16) if part.dtype == jnp.float32 else part

    return jax.tree.map(short, x)


def angles_of(positions, head_size):
    frequency = jnp.exp(
        jnp.arange(0, head_size, 2, dtype=jnp.float32) * (-math.log(rope_base) / head_size)
    )
    return positions.astype(jnp.float32)[:, None] * frequency[None, :]


def rotate(field, angles):
    half_size = field.shape[-1] // 2
    cosine = jnp.cos(angles)[:, None, :]
    sine_part = jnp.sin(angles)[:, None, :]
    first_half = field[..., :half_size]
    second = field[..., half_size:]
    return jnp.concatenate(
        [first_half * cosine - second * sine_part, second * cosine + first_half * sine_part],
        axis=-1,
    )


def unrotate(grad_field, angles):
    half_size = grad_field.shape[-1] // 2
    cosine = jnp.cos(angles)[:, None, :]
    sine_part = jnp.sin(angles)[:, None, :]
    first_half = grad_field[..., :half_size]
    second = grad_field[..., half_size:]
    return jnp.concatenate(
        [first_half * cosine + second * sine_part, second * cosine - first_half * sine_part],
        axis=-1,
    )


def block_positions(block_order, owner, half_rows):
    columns = lax.dynamic_slice_in_dim(block_order, 2 * owner, 2, 1)
    offsets = jnp.arange(half_rows, dtype=jnp.int32)
    return (columns[:, :, None] * half_rows + offsets[None, None, :]).reshape(
        columns.shape[0], 2 * half_rows
    )


def norm_back(values, inverse, gain, grad_normed):
    scaled = grad_normed * gain
    grad_gain = jnp.sum(grad_normed * values * inverse, axis=0)
    cubed = inverse * inverse * inverse
    grad_values = inverse * scaled - values * cubed * jnp.mean(
        values * scaled, axis=-1, keepdims=True
    )
    return (grad_values, grad_gain)


def make_rows_term(left_qkv, right_qkv, left_out, right_out, left_gu, right_gu):
    return jnp.concatenate(
        [
            jnp.einsum("rd,rc->dc", left_qkv, right_qkv, preferred_element_type=jnp.float32),
            jnp.einsum("rd,rc->dc", left_out, right_out, preferred_element_type=jnp.float32),
            jnp.einsum("rd,rc->dc", left_gu, right_gu, preferred_element_type=jnp.float32),
        ],
        axis=1,
    )


def make_down_term(left_hidden, right_grad):
    return jnp.einsum("rf,rd->fd", left_hidden, right_grad, preferred_element_type=jnp.float32)


def shards(
    hidden_in, block_order, attn_gain, w_qkv, b_qkv, w_out, mlp_gain, w_gate_up, w_down, cotangent
):
    w_qkv_all, w_out_all, bias_all, gain_first, gain_second = (
        lax.all_gather(w_qkv, "fsdp", axis=0, tiled=True),
        lax.all_gather(w_out, "fsdp", axis=0, tiled=True),
        lax.all_gather(b_qkv, "fsdp", axis=0, tiled=True),
        lax.all_gather(attn_gain, "fsdp", axis=0, tiled=True),
        lax.all_gather(mlp_gain, "fsdp", axis=0, tiled=True),
    )
    w_gu_all, w_down_all = (
        lax.all_gather(w_gate_up, "fsdp", axis=0, tiled=True),
        lax.all_gather(w_down, "fsdp", axis=0, tiled=True),
    )
    seq_count = hidden_in.shape[0]
    rows_dev = hidden_in.shape[1]
    ctx_count = lax.axis_size("ctx")
    ctx_index = lax.axis_index("ctx")
    half_rows = rows_dev // 2
    row_count = seq_count * rows_dev
    kv_width = KVH * HD
    head_group = H // KVH
    qkv_width = w_qkv.shape[1]
    score_scale = 1.0 / math.sqrt(HD)
    resid = hidden_in.reshape(row_count, D).astype(jnp.float32)
    own_pos = block_positions(block_order, ctx_index, half_rows)
    angles = angles_of(own_pos.reshape(row_count), HD)
    gain_one = gain_first.astype(jnp.float32)
    gain_two = gain_second.astype(jnp.float32)
    inv_first = lax.rsqrt(jnp.mean(resid * resid, axis=-1, keepdims=True) + eps)
    normed_in = (resid * inv_first * gain_one).astype(jnp.bfloat16)
    projected = jnp.dot(normed_in, w_qkv_all, preferred_element_type=jnp.float32) + bias_all.astype(
        jnp.float32
    )
    queries = rotate(projected[:, :D].reshape(row_count, H, HD), angles).astype(jnp.bfloat16)
    keys_own = (
        rotate(projected[:, D : D + kv_width].reshape(row_count, KVH, HD), angles)
        .astype(jnp.bfloat16)
        .reshape(seq_count, rows_dev, kv_width)
    )
    values_own = (
        projected[:, D + kv_width :].astype(jnp.bfloat16).reshape(seq_count, rows_dev, kv_width)
    )
    kept_keys = [keys_own]
    kept_values = [values_own]
    kept_pos = [own_pos]
    moving = (keys_own, values_own)
    for offset in range(1, ctx_count):
        moving = passed_along((moving[0], moving[1]), "ctx", 1)
        kept_keys.append(moving[0])
        kept_values.append(moving[1])
        kept_pos.append(block_positions(block_order, (ctx_index - offset) % ctx_count, half_rows))
    keys_all = jnp.concatenate(kept_keys, axis=1)
    values_all = jnp.concatenate(kept_values, axis=1)
    pos_all = jnp.concatenate(kept_pos, axis=1)
    query_heads = queries.reshape(seq_count, rows_dev, KVH, head_group, HD)
    key_heads = keys_all.reshape(seq_count, -1, KVH, HD)
    value_heads = values_all.reshape(seq_count, -1, KVH, HD)
    visible = own_pos[:, None, None, :, None] >= pos_all[:, None, None, None, :]

    def masked_scores():
        scores = (
            jnp.einsum(
                "sqkgd,snkd->skgqn", query_heads, key_heads, preferred_element_type=jnp.float32
            )
            * score_scale
        )
        return jnp.where(visible, scores, masked_value)

    scores = masked_scores()
    row_max = jnp.max(scores, axis=-1, keepdims=True)
    exponent = jnp.exp(scores - row_max)
    row_total = jnp.sum(exponent, axis=-1, keepdims=True)
    log_total = row_max + jnp.log(row_total)
    probability = (exponent / row_total).astype(jnp.bfloat16)
    attended = (
        jnp.einsum(
            "skgqn,snkd->sqkgd", probability, value_heads, preferred_element_type=jnp.float32
        )
        .reshape(row_count, D)
        .astype(jnp.bfloat16)
    )
    middle = resid + jnp.dot(attended, w_out_all, preferred_element_type=jnp.float32)
    inv_second = lax.rsqrt(jnp.mean(middle * middle, axis=-1, keepdims=True) + eps)
    normed_mid = (middle * inv_second * gain_two).astype(jnp.bfloat16)
    gate_up = jnp.dot(normed_mid, w_gu_all, preferred_element_type=jnp.float32)
    gate_part = gate_up[:, :FF]
    up_part = gate_up[:, FF:]
    sigmoid_gate = jax.nn.sigmoid(gate_part)
    silu_gate = gate_part * sigmoid_gate
    hidden = (silu_gate * up_part).astype(jnp.bfloat16)
    hidden_out = middle + jnp.dot(hidden, w_down_all, preferred_element_type=jnp.float32)
    grad_out = cotangent.reshape(row_count, D).astype(jnp.float32)
    grad_mlp = grad_out.astype(jnp.bfloat16)
    grad_act = jnp.einsum("rd,fd->rf", grad_mlp, w_down_all, preferred_element_type=jnp.float32)
    grad_gate = grad_act * up_part * sigmoid_gate * (1.0 + gate_part * (1.0 - sigmoid_gate))
    grad_up = grad_act * silu_gate
    grad_gu = jnp.concatenate([grad_gate, grad_up], axis=1).astype(jnp.bfloat16)
    grad_hn = jnp.einsum("rc,dc->rd", grad_gu, w_gu_all, preferred_element_type=jnp.float32)
    grad_mid_norm, grad_gain_two = norm_back(middle, inv_second, gain_two, grad_hn)
    grad_middle = grad_out + grad_mid_norm
    grad_attn = grad_middle.astype(jnp.bfloat16)
    grad_attended = jnp.einsum(
        "re,de->rd", grad_attn, w_out_all, preferred_element_type=jnp.float32
    ).astype(jnp.bfloat16)
    grad_heads = grad_attended.reshape(seq_count, rows_dev, KVH, head_group, HD)
    probs_again = jnp.exp(masked_scores() - log_total)
    grad_prob = jnp.einsum(
        "sqkgd,snkd->skgqn", grad_heads, value_heads, preferred_element_type=jnp.float32
    )
    grad_scores = (
        probs_again * (grad_prob - jnp.sum(probs_again * grad_prob, axis=-1, keepdims=True))
    ).astype(jnp.bfloat16)
    grad_query = (
        jnp.einsum("skgqn,snkd->sqkgd", grad_scores, key_heads, preferred_element_type=jnp.float32)
        * score_scale
    )
    grad_keys = (
        jnp.einsum(
            "skgqn,sqkgd->snkd", grad_scores, query_heads, preferred_element_type=jnp.float32
        )
        * score_scale
    )
    grad_values = jnp.einsum(
        "skgqn,sqkgd->snkd", probability, grad_heads, preferred_element_type=jnp.float32
    )
    key_pieces = grad_keys.reshape(seq_count, ctx_count, rows_dev, kv_width)
    value_pieces = grad_values.reshape(seq_count, ctx_count, rows_dev, kv_width)
    carried = (key_pieces[:, 1 % ctx_count], value_pieces[:, 1 % ctx_count])
    for offset in range(1, ctx_count):
        carried = (
            passed_along(as_sent(carried[0]), "ctx", 1),
            passed_along(carried[1].astype(jnp.bfloat16), "ctx", 1).astype(jnp.float32),
        )
        slot_index = (offset + 1) % ctx_count
        carried = (carried[0] + key_pieces[:, slot_index], carried[1] + value_pieces[:, slot_index])
    own_grad_keys, own_grad_values = carried
    grad_q_rows = unrotate(grad_query.reshape(row_count, H, HD), angles).reshape(row_count, D)
    grad_k_rows = unrotate(own_grad_keys.reshape(row_count, KVH, HD), angles).reshape(
        row_count, kv_width
    )
    grad_v_rows = own_grad_values.reshape(row_count, kv_width)
    grad_qkv = jnp.concatenate([grad_q_rows, grad_k_rows, grad_v_rows], axis=1).astype(jnp.bfloat16)
    grad_bias = jnp.sum(grad_qkv.astype(jnp.float32), axis=0)
    grad_xn = jnp.einsum("rc,dc->rd", grad_qkv, w_qkv_all, preferred_element_type=jnp.float32)
    grad_in_norm, grad_gain_one = norm_back(resid, inv_first, gain_one, grad_xn)
    grad_in = grad_middle + grad_in_norm
    down_part = lax.psum_scatter(
        make_down_term(hidden, grad_mlp).astype(jnp.bfloat16),
        "fsdp",
        scatter_dimension=0,
        tiled=True,
    )
    rows_part = lax.psum_scatter(
        make_rows_term(normed_in, grad_qkv, attended, grad_attn, normed_mid, grad_gu).astype(
            jnp.bfloat16
        ),
        "fsdp",
        scatter_dimension=0,
        tiled=True,
    )
    small_parts = (
        lax.psum_scatter(grad_gain_one, "fsdp", scatter_dimension=0, tiled=True),
        lax.psum_scatter(grad_gain_two, "fsdp", scatter_dimension=0, tiled=True),
        lax.psum_scatter(grad_bias, "fsdp", scatter_dimension=0, tiled=True),
    )
    totals = (
        lax.psum(rows_part, "ctx").astype(jnp.float32),
        lax.psum(down_part, "ctx").astype(jnp.float32),
        lax.psum(small_parts[0].astype(jnp.bfloat16), "ctx").astype(jnp.float32),
        lax.psum(small_parts[1].astype(jnp.bfloat16), "ctx").astype(jnp.float32),
        lax.psum(small_parts[2].astype(jnp.bfloat16), "ctx").astype(jnp.float32),
    )
    rows_total = totals[0]
    return (
        hidden_out.reshape(seq_count, rows_dev, D),
        grad_in.reshape(seq_count, rows_dev, D),
        totals[2],
        rows_total[:, :qkv_width],
        totals[4],
        rows_total[:, qkv_width : qkv_width + D],
        totals[3],
        rows_total[:, qkv_width + D :],
        totals[1],
    )


def solution(mesh):
    return jax.shard_map(
        shards,
        mesh=mesh,
        in_specs=(
            P("fsdp", "ctx", None),
            P("fsdp", None),
            P("fsdp"),
            P("fsdp", None),
            P("fsdp"),
            P("fsdp", None),
            P("fsdp"),
            P("fsdp", None),
            P("fsdp", None),
            P("fsdp", "ctx", None),
        ),
        out_specs=(
            P("fsdp", "ctx", None),
            P("fsdp", "ctx", None),
            P("fsdp"),
            P("fsdp", None),
            P("fsdp"),
            P("fsdp", None),
            P("fsdp"),
            P("fsdp", None),
            P("fsdp", None),
        ),
        check_vma=False,
    )
```

profile of v0, /device:TPU:6, one launch (start us, length us, event | category | flops | bytes accessed | tf_op | source)
XLA Modules:
  0.0 1551.3 jit_solution(6174689389813418338)
XLA Ops:
  16.4 38.5 %all-reduce.6 = (bf16[1536]{0:T(1024)(128)(2,1)S(1)}, bf16[1536]{0:T(1024)(128)(2,1)S(1)}) all-reduce(bf16[1536]{0:T(1024)(128)(2,1)S(1)} %dynamic-update-slice, bf16[1536]{0:T(1024)(128)(2,1)S(1)} %dynamic-update-slice.1), channel_id=1, replica_groups=mesh['ctx'=8,'fsdp'=16] {'fsdp'}, use_global_device_ids=true, to_apply=%add | all-reduce | flops 3072 | bytes 12288
  54.9 19.1 %all-gather = bf16[16,1,128]{2,1,0:T(2,128)(2,1)S(1)} all-gather(bf16[1,1,128]{2,1,0:T(2,128)(2,1)} %bitcast.350), channel_id=1, replica_groups=mesh['ctx'=8,'fsdp'=16] {'fsdp'}, dimensions={0}, use_global_device_ids=true | all-gather | bytes 4352 | tf_op jit(solution)/shard_map/all_gather | solution.py:104
  75.8 3.8 convolution_add_fusion.2
  86.3 3.0 collective-permute-start.1
  89.4 5.8 collective-permute-done.8
  95.5 2.4 collective-permute-start.2
  98.1 4.1 collective-permute-done.9
  105.5 4.1 collective-permute-done.10
  111.9 8.2 collective-permute-done.11
  120.8 9.8 collective-permute-done.12
  131.5 6.3 collective-permute-done.13
  143.8 3.4 multiply_reduce_fusion.2
  147.1 278.7 %all-gather.10.cloned.1.call-done = bf16[1536,17920]{1,0:T(8,128)(2,1)} async-done(((bf16[96,17920]{1,0:T(8,128)(2,1)}), bf16[1536,17920]{1,0:T(8,128)(2,1)}) %all-gather.10.cloned.1.call-update) | async-done | bytes 55050256 | tf_op jit(solution)/shard_map/all_gather | solution.py:109
  425.8 24.9 %fusion.90 = f32[128,17920]{1,0:T(8,128)} fusion(bf16[1536,17920]{1,0:T(8,128)(2,1)} %all-gather.10.cloned.1.call-done, f32[128,1536]{1,0:T(8,128)S(1)} %get-tuple-element.73, f32[1536]{0:T(1024)S(1)} %convert_element_type.229, f32[128]{0:T(128)S(1)} %get-tuple-element.61), kind=kOutput, calls=%fused_computation.195 | convolution fusion | flops 7047020544 | bytes 65018368 | tf_op jit(solution)/shard_map/dot_general | solution.py:183
  450.7 133.2 %all-gather.12.cloned.1.call-done = bf16[8960,1536]{1,0:T(8,128)(2,1)} async-done(((bf16[560,1536]{1,0:T(8,128)(2,1)}), bf16[8960,1536]{1,0:T(8,128)(2,1)}) %all-gather.12.cloned.1.call-update) | async-done | bytes 27525136 | tf_op jit(solution)/shard_map/all_gather | solution.py:110
  583.9 18.6 %multiply_convert_fusion.1 = (bf16[128,8960]{1,0:T(8,128)(2,1)}, bf16[128,8960]{1,0:T(8,128)(2,1)}, bf16[128,8960]{1,0:T(8,128)(2,1)}) fusion(f32[128,17920]{1,0:T(8,128)} %fusion.90, bf16[8960,1536]{1,0:T(8,128)(2,1)} %all-gather.12.cloned.1.call-done, bf16[1,128,1536]{2,1,0:T(8,128)(2,1)S(1)} %copy-done.14), kind=kOutput, calls=%fused_computation.17 | convolution fusion | flops 3540418560 | bytes 43974656 | tf_op jit(solution)/shard_map/rd,fd->rf/dot_general | solution.py:192
  602.5 14.6 convolution_convert_fusion.1
  617.8 33.9 %multiply_reduce_fusion = (f32[1536]{0:T(1024)}, f32[128]{0:T(128)S(1)}, f32[128,1536]{1,0:T(8,128)}) fusion(f32[128,1536]{1,0:T(8,128)S(1)} %get-tuple-element.73, f32[128]{0:T(128)S(1)} %get-tuple-element.61, f32[1536]{0:T(1024)S(1)} %convert_element_type.229, bf16[1536,17920]{1,0:T(8,128)(2,1)} %all-gather.10.cloned.1.call-done, ...), kind=kOutput, calls=%fused_computation.53 | convolution fusion | flops 7056783872 | bytes 61223936 | tf_op jit(solution)/shard_map/rc,dc->rd/dot_general | solution.py:196
  653.2 4.5 convolution_convert_fusion.4
  658.0 4.8 fusion.7
  664.4 4.0 convolution_convert_fusion.3
  668.5 7.1 copy.213
  675.6 5.1 fusion
  682.8 2.3 fusion.13
  686.1 2.3 collective-permute-start.14
  691.8 24.3 %convolution_convert_fusion = bf16[1536,17920]{1,0:T(8,128)(2,1)} fusion(bf16[128,8960]{1,0:T(8,128)(2,1)} %get-tuple-element.26, bf16[128,8960]{1,0:T(8,128)(2,1)} %get-tuple-element.25, f32[128,1536]{1,0:T(8,128)S(1)} %get-tuple-element.73, f32[1536]{0:T(1024)S(1)} %convert_element_type.229, f32[128]{0:T(128)S(1)} %copy-done.22), kind=kOutput, calls=%fused_computation | convolution fusion | flops 7083720704 | bytes 60430848 | tf_op jit(solution)/shard_map/rd,rc->dc/dot_general | solution.py:88
  718.7 2.3 collective-permute-start.22
  724.0 2.3 collective-permute-start.23
  728.2 2.4 collective-permute-start.17
  730.7 2.4 collective-permute-start.24
  733.0 3.3 collective-permute-done.17
  740.5 3.9 collective-permute-done.18
  744.6 2.7 collective-permute-done.25
  747.8 3.7 collective-permute-done.19
  751.6 2.3 collective-permute-done.26
  755.1 3.0 collective-permute-done.20
  758.7 3.1 collective-permute-done.27
  761.8 5.3 convolution_convert_fusion.2
  767.0 44.3 %pad_maximum_fusion = bf16[1536,21504]{1,0:T(8,128)(2,1)} fusion(bf16[1536,17920]{1,0:T(8,128)(2,1)} %convolution_convert_fusion, bf16[1536,1536]{1,0:T(8,128)(2,1)} %copy.213, bf16[1536,2048]{1,0:T(8,128)(2,1)} %convolution_convert_fusion.2), kind=kLoop, calls=%fused_computation.1 | loop fusion | flops 198180864 | bytes 132120576 | tf_op jit(solution)/shard_map/concatenate | solution.py:84
  811.4 18.9 %reduce-scatter.5.cloned.1.call-done = bf16[560,1536]{1,0:T(8,128)(2,1)} async-done(((bf16[8960,1536]{1,0:T(8,128)(2,1)}), bf16[560,1536]{1,0:T(8,128)(2,1)}) %reduce-scatter.5.cloned.1.call-update) | async-done | bytes 1720336 | tf_op jit(solution)/shard_map/reduce_scatter | solution.py:245
  830.3 452.6 %reduce-scatter.3.cloned.1.call-done = bf16[96,21504]{1,0:T(8,128)(2,1)} async-done(((bf16[1536,21504]{1,0:T(8,128)(2,1)}), bf16[96,21504]{1,0:T(8,128)(2,1)}) %reduce-scatter.3.cloned.1.call-update) | async-done | bytes 4128784 | tf_op jit(solution)/shard_map/reduce_scatter | solution.py:251
  1284.3 14.1 fusion.12
  1298.6 5.2 fusion.26
  1303.8 68.7 %all-reduce.5 = (bf16[1536]{0:T(1024)(128)(2,1)S(1)}, bf16[2048]{0:T(1024)(128)(2,1)S(1)}, bf16[1536]{0:T(1024)(128)(2,1)S(1)}) all-reduce(f32[1536]{0:T(1024)S(1)} %get-tuple-element.11, f32[2048]{0:T(1024)S(1)} %convert_reduce_fusion, f32[1536]{0:T(1024)S(1)} %copy-done.24), channel_id=2, replica_groups=mesh['ctx'=8,'fsdp'=16] {'fsdp'}, use_global_device_ids=true, to_apply=%region_8.9.clone | all-reduce | flops 5120 | bytes 30720
  1372.7 17.7 %all-reduce.7 = (bf16[96]{0:T(256)(128)(2,1)S(1)}, bf16[128]{0:T(256)(128)(2,1)S(1)}, bf16[96]{0:T(256)(128)(2,1)S(1)}) all-reduce(bf16[96]{0:T(256)(128)(2,1)S(1)} %dynamic-slice.13, bf16[128]{0:T(256)(128)(2,1)S(1)} %dynamic-slice.12, bf16[96]{0:T(256)(128)(2,1)S(1)} %dynamic-slice.11), channel_id=1, replica_groups=mesh['ctx'=8,'fsdp'=16] {'ctx'}, use_global_device_ids=true, to_apply=%region_9.10 | all-reduce | flops 320 | bytes 1280 | tf_op jit(solution)/shard_map/psum | solution.py:267
  1393.2 139.3 %all-reduce.11.cloned.1.call-done = (bf16[96,21504]{1,0:T(8,128)(2,1)}, bf16[560,1536]{1,0:T(8,128)(2,1)}) async-done(((bf16[96,21504]{1,0:T(8,128)(2,1)}, bf16[560,1536]{1,0:T(8,128)(2,1)}), (bf16[96,21504]{1,0:T(8,128)(2,1)}, bf16[560,1536]{1,0:T(8,128)(2,1)})) %all-reduce.11.cloned.1.call-update) | async-done | bytes 5849104 | tf_op jit(solution)/shard_map/psum | solution.py:265
  1536.3 5.6 slice.162
  1541.8 2.2 convert_element_type.273
  (254 shorter events, 61.9 us)
Async XLA Ops:
  7.2 67.3 %copy-start.3 = (bf16[1,128,1536]{2,1,0:T(8,128)(2,1)S(1)}, bf16[1,128,1536]{2,1,0:T(8,128)(2,1)}, u32[]{:S(2)}) copy-start(bf16[1,128,1536]{2,1,0:T(8,128)(2,1)} %param.10) | copy-start | bytes 1179652
  7.2 68.7 %all-gather.6.cloned.1.call-start = ((), (), s32[]{:S(2)}) async-start(), calls=%async_computation.2 | async-start | bytes 6684672 | tf_op jit(solution)/shard_map/all_gather | solution.py:102
  7.9 135.8 %all-gather.8.cloned.1.call-start = ((), (), s32[]{:S(2)}) async-start(), calls=%async_computation.3 | async-start | bytes 5013504 | tf_op jit(solution)/shard_map/all_gather | solution.py:103
  8.7 417.1 %all-gather.10.cloned.1.call-start = ((), (), s32[]{:S(2)}) async-start(), calls=%async_computation.4 | async-start | bytes 58490880 | tf_op jit(solution)/shard_map/all_gather | solution.py:109
  9.4 574.5 %all-gather.12.cloned.1.call-start = ((), (), s32[]{:S(2)}) async-start(), calls=%async_computation.5 | async-start | bytes 29245440 | tf_op jit(solution)/shard_map/all_gather | solution.py:110
  10.0 820.3 %reduce-scatter.5.cloned.1.call-start = ((), (), s32[]{:S(2)}) async-start(), calls=%async_computation.7 | async-start | bytes 29245440 | tf_op jit(solution)/shard_map/reduce_scatter | solution.py:245
  74.3 9.5 copy-start.17
  74.3 9.5 copy-start.19
  79.9 6.2 collective-permute-start
  81.7 4.3 collective-permute-start.7
  84.2 56.3 %copy-start.6 = (bf16[128,12,64]{2,0,1:T(8,128)(2,1)}, bf16[128,12,64]{2,0,1:T(8,128)(2,1)S(1)}, u32[]{:S(2)}) copy-start(bf16[128,12,64]{2,0,1:T(8,128)(2,1)S(1)} %copy.183) | copy-start | bytes 589828
  84.4 56.1 %copy-start.8 = (bf16[128,12,64]{2,0,1:T(8,128)(2,1)}, bf16[128,12,64]{2,0,1:T(8,128)(2,1)S(1)}, u32[]{:S(2)}) copy-start(bf16[128,12,64]{2,0,1:T(8,128)(2,1)S(1)} %copy.184) | copy-start | bytes 589828
  86.3 9.1 collective-permute-start.1
  89.3 6.0 collective-permute-start.8
  95.5 6.8 collective-permute-start.2
  97.9 4.3 collective-permute-start.9
  102.4 7.3 collective-permute-start.3
  104.1 5.5 collective-permute-start.10
  109.8 10.4 collective-permute-start.4
  111.0 9.1 collective-permute-start.11
  120.3 10.3 collective-permute-start.5
  120.7 9.9 collective-permute-start.12
  130.8 7.1 collective-permute-start.6
  130.9 6.8 collective-permute-start.13
  143.7 307.0 %copy-start.9 = (bf16[2,128,6,128]{3,1,2,0:T(8,128)(2,1)}, bf16[2,128,6,128]{3,1,2,0:T(8,128)(2,1)S(1)}, u32[]{:S(2)}) copy-start(bf16[2,128,6,128]{3,1,2,0:T(8,128)(2,1)S(1)} %fusion.14) | copy-start | bytes 1179652
  147.1 504.5 %copy-start.21 = (f32[128]{0:T(128)}, f32[128]{0:T(128)S(1)}, u32[]{:S(2)}) copy-start(f32[128]{0:T(128)S(1)} %get-tuple-element.61) | copy-start | bytes 1540
  425.8 158.1 %copy-start.14 = (bf16[1,128,1536]{2,1,0:T(8,128)(2,1)S(1)}, bf16[1,128,1536]{2,1,0:T(8,128)(2,1)}, u32[]{:S(2)}) copy-start(bf16[1,128,1536]{2,1,0:T(8,128)(2,1)} %param.19) | copy-start | bytes 1179652
  617.1 665.8 %reduce-scatter.3.cloned.1.call-start = ((), (), s32[]{:S(2)}) async-start(), calls=%async_computation.6 | async-start | bytes 70189056 | tf_op jit(solution)/shard_map/reduce_scatter | solution.py:251
  653.2 11.2 copy-start.1
  663.9 53.9 %collective-permute-start.21 = (bf16[1,128,256]{1,2,0:T(8,128)(2,1)}, bf16[1,128,256]{1,2,0:T(8,128)(2,1)}, u32[]{:S(2)}, u32[]{:S(2)}) collective-permute-start(bf16[1,128,256]{1,2,0:T(8,128)(2,1)} %bitcast.304), channel_id=1, source_target_pairs={{112,0},{0,16},{16,32},{32,48},{48,64},{64,80},{80,96},{96,112},{1... | collective-permute-start | bytes 196616 | tf_op jit(solution)/shard_map/ppermute | solution.py:23
  668.5 12.2 slice-start
  686.1 30.0 %collective-permute-start.14 = (bf16[1,128,256]{1,2,0:T(8,128)(2,1)}, bf16[1,128,256]{1,2,0:T(8,128)(2,1)}, u32[]{:S(2)}, u32[]{:S(2)}) collective-permute-start(bf16[1,128,256]{1,2,0:T(8,128)(2,1)} %bitcast.303), channel_id=1, source_target_pairs={{112,0},{0,16},{16,32},{32,48},{48,64},{64,80},{80,96},{96,112},{1... | collective-permute-start | bytes 196616 | tf_op jit(solution)/shard_map/ppermute | solution.py:23
  717.1 4.6 collective-permute-start.15
  718.7 5.2 collective-permute-start.22
  722.6 5.6 collective-permute-start.16
  724.0 6.7 collective-permute-start.23
  728.2 8.1 collective-permute-start.17
  730.7 8.4 collective-permute-start.24
  736.3 8.0 collective-permute-start.18
  739.1 8.2 collective-permute-start.25
  744.4 7.2 collective-permute-start.19
  747.3 6.6 collective-permute-start.26
  751.6 6.6 collective-permute-start.20
  753.9 7.8 collective-permute-start.27
  811.4 721.1 %all-reduce.11.cloned.1.call-start = ((), (), s32[]{:S(2)}) async-start(), calls=%async_computation.8 | async-start | bytes 11698176 | tf_op jit(solution)/shard_map/psum | solution.py:265
  1284.3 14.4 copy-start.26
  1298.4 93.6 %copy-start.2 = (f32[128,1536]{1,0:T(8,128)S(1)}, f32[128,1536]{1,0:T(8,128)}, u32[]{:S(2)}) copy-start(f32[128,1536]{1,0:T(8,128)} %copy-done.1) | copy-start | bytes 2359300
  1298.4 93.6 %copy-start.27 = (f32[128]{0:T(128)S(1)}, f32[128]{0:T(128)}, u32[]{:S(2)}) copy-start(f32[128]{0:T(128)} %get-tuple-element.58) | copy-start | bytes 1540
  (17 other events, 74.4 us)
Sparse Core Ops, SparseCore 0:
  10.5 65.2 all-gather.5
  78.3 61.6 all-gather.7
  142.5 283.2 all-gather.9
  428.1 155.7 all-gather.11
  617.2 213.0 reduce-scatter.4
  835.5 447.3 reduce-scatter.2
  1285.5 246.8 all-reduce.10
where the time goes:
time: 1560 us; the launch traced here: 1550 us
  waiting for transfers between devices  1090 us (70%)
  matrix products  172 us (11%)
  blocking collectives  144 us (9%)
  other arithmetic  60.8 us (4%)
  starting transfers between devices  34.2 us (2%)
  local copies, waits for them, and re-layouts  31.3 us (2%)
  between operations  17.7 us (1%)
    reduce_scatter x1, waiting for transfers between devices, shards(): lax.psum_scatter(make_rows_term(normed_in, grad_qkv, attended, grad_attn,...  453 us
    all_gather x1, waiting for transfers between devices, shards(): lax.all_gather(w_gate_up, 'fsdp', axis=0, tiled=True)  279 us
    psum x1, waiting for transfers between devices, shards(): lax.psum(rows_part, 'ctx').astype(jnp.float32)  139 us
    all_gather x1, waiting for transfers between devices, shards(): lax.all_gather(w_down, 'fsdp', axis=0, tiled=True)  133 us
    unnamed x2, blocking collectives  107 us
    ppermute x28, waiting for transfers between devices, passed_along(): return lax.ppermute(block, axis, route)  65.5 us
    concatenate x1, other arithmetic, make_rows_term(): jnp.concatenate([jnp.einsum('rd,rc->dc', left_qkv, right_qkv, preferred_e...  44.3 us
    ppermute x28, starting transfers between devices, passed_along(): return lax.ppermute(block, axis, route)  34 us
  transfers between devices with their start and end apart: 35, of which 23 were waited for; matrix products, arithmetic and copies ran while one was open for 14% of the time, Pallas kernels for 0%

commit v1 on v0

v1 whole, which is shorter than its diff:
```python
import math

import jax
import jax.numpy as jnp
from jax import lax
from jax.sharding import Mesh, PartitionSpec as P

D = 1536
H = 12
KVH = 2
HD = 128
FF = 8960
SLICE = FF // 8
WIDE = 1152

CTX = ("y", "xl")
FSDP = ("xh", "z", "core")

eps = 1e-06
rope_base = 1000000.0
masked_value = -1e30
bf16 = jnp.bfloat16
f32 = jnp.float32


def moved(block, ring, pair, step, flip):
    size = lax.axis_size(ring)
    if step == 0:
        return lax.ppermute(block, pair, [(0, 1), (1, 0)])
    return lax.ppermute(block, ring, [(i, (i + step) % size) for i in range(size)])


def gather_eight(block, ring, pair):
    rows = block.shape[0]
    half = rows // 2
    across = moved(block, ring, pair, 0, 1)
    before = moved(block, ring, pair, 1, 0)
    after = moved(block, ring, pair, -1, 0)
    far_first = moved(before[:half], ring, pair, 1, 0)
    far_second = moved(after[half:], ring, pair, -1, 0)
    across_before = moved(across, ring, pair, 1, 0)
    across_after = moved(across, ring, pair, -1, 0)
    across_far_first = moved(far_first, ring, pair, 0, 1)
    across_far_second = moved(far_second, ring, pair, 0, 1)
    return [
        (0, 0, 0, block),
        (0, 1, 0, across),
        (-1, 0, 0, before),
        (1, 0, 0, after),
        (-1, 1, 0, across_before),
        (1, 1, 0, across_after),
        (2, 0, 0, far_first),
        (2, 0, half, far_second),
        (2, 1, 0, across_far_first),
        (2, 1, half, across_far_second),
    ]


def place(ring, pair, ring_major, step, flip):
    size = lax.axis_size(ring)
    r = (lax.axis_index(ring) + step) % size
    q = lax.axis_index(pair)
    q = 1 - q if flip else q
    return r * 2 + q if ring_major else q * size + r


def gathered(block, ring, pair, ring_major):
    rows = block.shape[0]
    whole = jnp.zeros((8 * rows,) + block.shape[1:], block.dtype)
    for step, flip, first, piece in gather_eight(block, ring, pair):
        at = place(ring, pair, ring_major, step, flip) * rows + first
        whole = lax.dynamic_update_slice_in_dim(whole, piece, at, 0)
    return whole


def scattered(parts, ring, pair, ring_major):
    half = parts.shape[1] // 2

    def part(step, flip):
        at = place(ring, pair, ring_major, step, flip)
        return lax.dynamic_index_in_dim(parts, at, 0, keepdims=False)

    def add(a, b):
        return (a.astype(f32) + b.astype(f32)).astype(bf16)

    far_across = moved(part(2, 1), ring, pair, 0, 1)
    from_after = moved(part(-1, 1), ring, pair, -1, 0)
    from_before = moved(part(1, 1), ring, pair, 1, 0)
    far = part(2, 0)
    far_first = moved(add(far[:half], far_across[:half]), ring, pair, -1, 0)
    far_second = moved(add(far[half:], far_across[half:]), ring, pair, 1, 0)
    across = part(0, 1)
    across = (across.astype(f32) + from_after.astype(f32) + from_before.astype(f32)).astype(bf16)
    got_across = moved(across, ring, pair, 0, 1)
    back = part(-1, 0)
    back = jnp.concatenate([add(back[:half], far_first), back[half:]], axis=0)
    ahead = part(1, 0)
    ahead = jnp.concatenate([ahead[:half], add(ahead[half:], far_second)], axis=0)
    got_back = moved(back, ring, pair, -1, 0)
    got_ahead = moved(ahead, ring, pair, 1, 0)
    return (
        part(0, 0).astype(f32)
        + got_across.astype(f32)
        + got_back.astype(f32)
        + got_ahead.astype(f32)
    )


def swap_core(block):
    return lax.ppermute(block, "core", [(0, 1), (1, 0)])


def gathered_fsdp(block):
    rows, columns = block.shape
    own = gathered(block, "z", "xh", False)
    other = swap_core(own)
    own = own.reshape(8, rows, columns)
    other = other.reshape(8, rows, columns)
    first = lax.axis_index("core") == 0
    return jnp.stack(
        [jnp.where(first, own, other), jnp.where(first, other, own)], axis=1
    ).reshape(16 * rows, columns)


def scattered_fsdp(parts):
    _, rows, columns = parts.shape
    core = lax.axis_index("core")
    pairs = parts.reshape(8, 2, rows, columns)
    given = lax.dynamic_index_in_dim(pairs, 1 - core, 1, keepdims=False)
    kept = lax.dynamic_index_in_dim(pairs, core, 1, keepdims=False)
    got = swap_core(given)
    both = (kept.astype(f32) + got.astype(f32)).astype(bf16)
    return scattered(both, "z", "xh", False)


def scattered_ctx(part):
    pieces = lax.all_to_all(part.reshape(8, 128, D), CTX, 0, 0, tiled=True)
    return jnp.sum(pieces.astype(f32), axis=0)


def rotate(field, cosine, sine):
    half = field.shape[-1] // 2
    a, b = field[..., :half], field[..., half:]
    return jnp.concatenate([a * cosine - b * sine, b * cosine + a * sine], axis=-1)


def unrotate(field, cosine, sine):
    half = field.shape[-1] // 2
    a, b = field[..., :half], field[..., half:]
    return jnp.concatenate([a * cosine + b * sine, b * cosine - a * sine], axis=-1)


def mm(a, b):
    return jnp.dot(a, b, preferred_element_type=f32)


def mm_nt(a, b):
    return jnp.einsum("ik,jk->ij", a, b, preferred_element_type=f32)


def mm_tn(a, b):
    return jnp.einsum("ki,kj->ij", a, b, preferred_element_type=f32)


def own_half(rows, half):
    n = rows.shape[-1]
    return lax.dynamic_index_in_dim(
        rows.reshape(8, 2, 64, n), half, 1, keepdims=False
    ).reshape(512, n)


def shards(
    hidden_in, block_order, attn_gain, w_qkv, b_qkv, w_out, mlp_gain, w_gate_up, w_down, cotangent
):
    yi, qi = lax.axis_index("y"), lax.axis_index("xl")
    ci = 2 * yi + qi
    fi = lax.axis_index(FSDP)
    group = yi // 2
    x_own = hidden_in[0]
    cot_own = cotangent[0]

    starts = (
        HD * (3 * yi + 2 * qi),
        HD * (3 * yi + 1),
        D + HD * group,
        D + HD * (KVH + group),
    )

    def my_columns(array):
        return jnp.concatenate(
            [lax.dynamic_slice_in_dim(array, s, HD, array.ndim - 1) for s in starts], axis=-1
        )

    bias_low = jnp.concatenate([b_qkv[:96, None], jnp.pad(b_qkv[96:], (0, 64))[:, None]], axis=1)
    extra = jnp.concatenate([attn_gain[:, None], mlp_gain[:, None], bias_low], axis=1)
    extra = jnp.pad(extra, ((0, 0), (0, 124)))
    packed = jnp.concatenate([my_columns(w_qkv), w_out, extra], axis=1)

    x_all = gathered(x_own, "y", "xl", True)
    packed_all = gathered_fsdp(packed)

    pad = jnp.zeros((96, WIDE - SLICE), bf16)
    gu_own = jnp.concatenate(
        [
            lax.dynamic_slice_in_dim(w_gate_up, SLICE * ci, SLICE, 1),
            pad,
            lax.dynamic_slice_in_dim(w_gate_up, FF + SLICE * ci, SLICE, 1),
            pad,
        ],
        axis=1,
    )
    w_gu = lax.all_gather(gu_own, FSDP, axis=0, tiled=True)
    whole = CTX + FSDP
    route = [
        ((s % 8) * 16 + 2 * c + s // 8, c * 16 + s) for c in range(8) for s in range(16)
    ]
    wd_own = lax.ppermute(lax.dynamic_slice_in_dim(w_down, 70 * ci, 70, 0), whole, route)
    w_dn = lax.all_gather(wd_own, FSDP, axis=0, tiled=True)
    w_qkv_all = lax.all_gather(w_qkv, FSDP, axis=0, tiled=True)
    cot_all = gathered(cot_own, "y", "xl", True)

    w_mine = packed_all[:, :512]
    w_out_all = packed_all[:, 512 : 512 + D]
    extras = packed_all[:, 512 + D :].astype(f32)
    gain_one = extras[:, 0]
    gain_two = extras[:, 1]
    bias_rows = extras.reshape(16, 96, 128)
    bias_all = jnp.concatenate([bias_rows[:, :, 2], bias_rows[:, :32, 3]], axis=1).reshape(2048)
    bias_mine = my_columns(bias_all)

    order = block_order[0]
    positions = (order[:, None] * 64 + jnp.arange(64, dtype=jnp.int32)[None, :]).reshape(1024)
    frequency = jnp.exp(jnp.arange(0, HD, 2, dtype=f32) * (-math.log(rope_base) / HD))
    angles = positions.astype(f32)[:, None] * frequency[None, :]
    cosine, sine = jnp.cos(angles), jnp.sin(angles)
    score_scale = 1.0 / math.sqrt(HD)

    resid_all = x_all.astype(f32)
    inv_all = lax.rsqrt(jnp.mean(resid_all * resid_all, axis=-1, keepdims=True) + eps)
    normed_all = (resid_all * inv_all * gain_one).astype(bf16)
    projected = mm(normed_all, w_mine) + bias_mine
    q_a = rotate(projected[:, :HD], cosine, sine).astype(bf16)
    q_b = rotate(projected[:, HD : 2 * HD], cosine, sine).astype(bf16)
    keys = rotate(projected[:, 2 * HD : 3 * HD], cosine, sine).astype(bf16)
    values = projected[:, 3 * HD :].astype(bf16)
    queries = jnp.concatenate([q_a, own_half(q_b, qi)], axis=0)
    q_pos = jnp.concatenate(
        [positions, lax.dynamic_index_in_dim(positions.reshape(8, 2, 64), qi, 1, False).reshape(512)]
    )
    scores = mm_nt(queries, keys) * score_scale
    scores = jnp.where(q_pos[:, None] >= positions[None, :], scores, masked_value)
    row_max = jnp.max(scores, axis=-1, keepdims=True)
    exponent = jnp.exp(scores - row_max)
    probs = exponent / jnp.sum(exponent, axis=-1, keepdims=True)
    probability = probs.astype(bf16)
    att_mine = mm(probability, values).astype(bf16)

    def to_rows(head_a, head_b):
        return jnp.concatenate([head_a.reshape(8, 128, HD), head_b.reshape(8, 64, HD)], axis=1)

    def rows_of(got):
        got = got.reshape(4, 2, 192, HD)
        first, last = got[:, 0, :128], got[:, 1, :128]
        mid = got[:, :, 128:].reshape(4, 128, HD)
        return jnp.stack([first, mid, last], axis=1).transpose(2, 0, 1, 3).reshape(128, D)

    got = lax.all_to_all(to_rows(att_mine[:1024], att_mine[1024:]), CTX, 0, 0, tiled=True)
    attended = rows_of(got)

    resid = x_own.astype(f32)
    inv_first = lax.rsqrt(jnp.mean(resid * resid, axis=-1, keepdims=True) + eps)
    middle = resid + mm(attended, w_out_all)
    inv_second = lax.rsqrt(jnp.mean(middle * middle, axis=-1, keepdims=True) + eps)
    normed_mid = (middle * inv_second * gain_two).astype(bf16)
    nm_all = gathered(normed_mid, "y", "xl", True)

    gate_up = mm(nm_all, w_gu)
    gate, up = gate_up[:, :SLICE], gate_up[:, WIDE : WIDE + SLICE]
    sigmoid_gate = jax.nn.sigmoid(gate)
    silu_gate = gate * sigmoid_gate
    hidden = (silu_gate * up).astype(bf16)
    grad_act = mm_nt(cot_all, w_dn)
    grad_gate = grad_act * up * sigmoid_gate * (1.0 + gate * (1.0 - sigmoid_gate))
    grad_up = grad_act * silu_gate
    zero = jnp.zeros((1024, WIDE - SLICE), bf16)
    grad_gu = jnp.concatenate([grad_gate.astype(bf16), zero, grad_up.astype(bf16), zero], axis=1)
    hn_part = mm_nt(grad_gu, w_gu).astype(bf16)
    out_part = mm(hidden, w_dn).astype(bf16)

    grad_hn = scattered_ctx(hn_part)
    hidden_sum = lax.psum_scatter(out_part, CTX, scatter_dimension=0, tiled=True)
    hidden_out = middle + hidden_sum.astype(f32)

    gw_dn = mm_tn(hidden, cot_all).astype(bf16)
    gw_gu = mm_tn(nm_all, grad_gu).astype(bf16)

    grad_out = cot_own.astype(f32)
    scaled = grad_hn * gain_two
    grad_middle = (
        grad_out
        + inv_second * scaled
        - middle * (inv_second**3) * jnp.mean(middle * scaled, axis=-1, keepdims=True)
    )
    grad_attn = grad_middle.astype(bf16)
    grad_attended = mm_nt(grad_attn, w_out_all).astype(bf16)
    by_head = grad_attended.reshape(128, 4, 3, HD)
    send_a = by_head[:, :, ::2].transpose(1, 2, 0, 3)
    send_b = by_head.reshape(2, 64, 4, 3, HD)[:, :, :, 1].transpose(2, 0, 1, 3)
    send = jnp.concatenate([send_a, send_b], axis=2).reshape(8, 192, HD)
    got = lax.all_to_all(send, CTX, 0, 0, tiled=True)
    grad_heads = jnp.concatenate(
        [got[:, :128].reshape(1024, HD), got[:, 128:].reshape(512, HD)], axis=0
    )

    grad_prob = mm_nt(grad_heads, values)
    grad_scores = (
        probs * (grad_prob - jnp.sum(probs * grad_prob, axis=-1, keepdims=True))
    ).astype(bf16)
    grad_q = mm(grad_scores, keys) * score_scale
    grad_k = mm_tn(grad_scores, queries) * score_scale
    grad_v = mm_tn(probability, grad_heads)
    half_cos = lax.dynamic_index_in_dim(cosine.reshape(8, 2, 64, 64), qi, 1, False).reshape(512, 64)
    half_sin = lax.dynamic_index_in_dim(sine.reshape(8, 2, 64, 64), qi, 1, False).reshape(512, 64)
    gp_a = unrotate(grad_q[:1024], cosine, sine).astype(bf16)
    gp_b = unrotate(grad_q[1024:], half_cos, half_sin).astype(bf16)
    gp_k = unrotate(grad_k, cosine, sine).astype(bf16)
    gp_v = grad_v.astype(bf16)

    send = jnp.concatenate(
        [
            to_rows(gp_a, gp_b),
            gp_k.reshape(8, 128, HD),
            gp_v.reshape(8, 128, HD),
        ],
        axis=1,
    )
    got = lax.all_to_all(send, CTX, 0, 0, tiled=True)
    gq_rows = rows_of(got[:, :192])
    gkv = jnp.sum(got[:, 192:].astype(f32).reshape(2, 4, 2, 128, HD), axis=1).astype(bf16)
    gkv_rows = gkv.transpose(2, 1, 0, 3).reshape(128, 4 * HD)
    gp_rows = jnp.concatenate([gq_rows, gkv_rows], axis=1)
    grad_xn = mm_nt(gp_rows, w_qkv_all)
    scaled = grad_xn * gain_one
    grad_in = (
        grad_middle
        + inv_first * scaled
        - resid * (inv_first**3) * jnp.mean(resid * scaled, axis=-1, keepdims=True)
    )

    here = (jnp.arange(2) == qi)[None, :, None, None]
    gp_b_all = jnp.where(here, gp_b.reshape(8, 1, 64, HD), jnp.zeros((), bf16)).reshape(1024, HD)
    gp_mine = jnp.concatenate([gp_a, gp_b_all, gp_k, gp_v], axis=1)
    gw_mine = mm_tn(normed_all, gp_mine).astype(bf16)
    gb_mine = jnp.sum(gp_mine.astype(f32), axis=0).astype(bf16)
    qkv_parts = jnp.concatenate(
        [gw_mine.reshape(16, 96, 512), jnp.broadcast_to(gb_mine, (16, 16, 512))], axis=1
    )
    qkv_sum = scattered_fsdp(qkv_parts).astype(bf16)

    gw_out = mm_tn(attended, grad_attn).astype(bf16)
    out_sum = scattered_fsdp(gw_out.reshape(16, 96, D)).astype(bf16)
    out_pieces = lax.all_to_all(
        out_sum.reshape(96, 8, 192).transpose(1, 0, 2), CTX, 0, 0, tiled=True
    )
    out_mine = jnp.sum(out_pieces.astype(f32), axis=0).astype(bf16)

    gu_sum = scattered_fsdp(gw_gu.reshape(16, 96, 2 * WIDE)).astype(bf16)
    dn_sum = lax.psum_scatter(gw_dn, FSDP, scatter_dimension=0, tiled=True)
    dn_mine = lax.ppermute(dn_sum, whole, [(b, a) for a, b in route])
    grad_w_down = lax.all_gather(dn_mine, CTX, axis=0, tiled=True).astype(f32)

    gu_all = gathered(gu_sum, "y", "xl", True).reshape(8, 96, 2 * WIDE)
    grad_w_gate_up = jnp.concatenate(
        [gu_all[c, :, :SLICE] for c in range(8)]
        + [gu_all[c, :, WIDE : WIDE + SLICE] for c in range(8)],
        axis=1,
    ).astype(f32)
    grad_mlp_gain = jnp.sum(grad_w_gate_up * w_gate_up.astype(f32), axis=1) / mlp_gain.astype(f32)

    tail = jnp.concatenate([qkv_sum, jnp.pad(out_mine, ((0, 16), (0, 64)))], axis=1)
    tail_all = gathered(tail, "y", "xl", True).reshape(8, 112, 768)
    grad_w_out = tail_all[:, :96, 512:704].transpose(1, 0, 2).reshape(96, D).astype(f32)
    qkv_all = tail_all[:, :, :512].astype(f32).reshape(4, 2, 112, 4, HD)
    head_first = qkv_all[:, 0, :, 0]
    head_last = qkv_all[:, 1, :, 0]
    head_mid = qkv_all[:, 0, :, 1] + qkv_all[:, 1, :, 1]
    gq = jnp.stack([head_first, head_mid, head_last], axis=1).reshape(12, 112, HD)
    gk = jnp.sum(qkv_all[:, :, :, 2].reshape(2, 4, 112, HD), axis=1)
    gv = jnp.sum(qkv_all[:, :, :, 3].reshape(2, 4, 112, HD), axis=1)
    heads = jnp.concatenate([gq, gk, gv], axis=0)
    grad_w_qkv = heads[:, :96].transpose(1, 0, 2).reshape(96, 2048)
    grad_b_qkv = lax.dynamic_index_in_dim(heads[:, 96], fi, 0, keepdims=False)
    grad_attn_gain = jnp.sum(grad_w_qkv * w_qkv.astype(f32), axis=1) / attn_gain.astype(f32)

    return (
        hidden_out[None],
        grad_in[None],
        grad_attn_gain,
        grad_w_qkv,
        grad_b_qkv,
        grad_w_out,
        grad_mlp_gain,
        grad_w_gate_up,
        grad_w_down,
    )


def solution(mesh):
    fine = Mesh(mesh.devices.reshape(4, 2, 2, 4, 2), CTX + FSDP)
    rows = P(FSDP, CTX, None)
    vector = P(FSDP)
    matrix = P(FSDP, None)
    return jax.shard_map(
        shards,
        mesh=fine,
        in_specs=(rows, matrix, vector, matrix, vector, matrix, vector, matrix, matrix, rows),
        out_specs=(rows, rows, vector, matrix, vector, matrix, vector, matrix, matrix),
        check_vma=False,
    )
```

time: 1560 us -> 753 us (0.48)
  waiting for transfers between devices: 1090 us -> 224 us
  starting transfers between devices: 34.2 us -> 160 us
  local copies, waits for them, and re-layouts: 31.3 us -> 131 us
  blocking collectives: 144 us -> 55.1 us
  matrix products: 172 us -> 95.9 us
    reduce_scatter x2 -> x1, waiting for transfers between devices: 472 us -> 0.01 us  [shards(): lax.psum_scatter(out_part, CTX, scatter_dimension=0, tiled=True)]
    all_gather x4, waiting for transfers between devices: 412 us -> 0.04 us  [the longest x1 0.02 us: shards(): w_qkv_all = lax.all_gather(w_qkv, FSDP, axis=0, tiled=True)]
    ppermute x28 -> x84, waiting for transfers between devices: 65.5 us -> 206 us  [the longest x24 90.9 us: moved(): return lax.ppermute(block, pair, [(0, 1), (1, 0)])]
    psum x1 -> x0, waiting for transfers between devices: 139 us -> none  [shards(): lax.psum(rows_part, 'ctx').astype(jnp.float32)]
    ppermute x28 -> x84, starting transfers between devices: 34 us -> 134 us  [the longest x54 99.7 us: moved(): lax.ppermute(block, ring, [(i, (i + step) % size) for i in range(size)])]
    dot_general x18, matrix products: 172 us -> 95.9 us  [the longest x6 37.4 us: mm_nt(): return jnp.einsum('ik,jk->ij', a, b, preferred_element_type=f32)]
    unnamed x2 -> x1, blocking collectives: 107 us -> 42.1 us
    concatenate x5 -> x16, other arithmetic: 44.5 us -> 4.16 us  [the longest x1 1.37 us: shards(): jnp.concatenate([to_rows(gp_a, gp_b), gp_k.reshape(8, 128, HD), gp_v.resh...]
  transfers between devices with their start and end apart: 35 -> 94, of which waited for: 23 -> 42; matrix products, arithmetic and copies ran while one was open for 14% -> 31% of each run, Pallas kernels for 0% -> 0%
where the time goes in v1:
time: 753 us; the launch traced here: 741 us
  waiting for transfers between devices  224 us (30%)
  starting transfers between devices  160 us (21%)
  local copies, waits for them, and re-layouts  131 us (17%)
  matrix products  95.9 us (13%)
  other arithmetic  58.3 us (8%)
  blocking collectives  55.1 us (7%)
  between operations  17 us (2%)
    ppermute x54, starting transfers between devices, moved(): lax.ppermute(block, ring, [(i, (i + step) % size) for i in range(size)])  99.7 us
    ppermute x24, waiting for transfers between devices, moved(): return lax.ppermute(block, pair, [(0, 1), (1, 0)])  90.9 us
    ppermute x54, waiting for transfers between devices, moved(): lax.ppermute(block, ring, [(i, (i + step) % size) for i in range(size)])  90.6 us
    unnamed x1, blocking collectives  42.1 us
    dynamic_update_slice x56, local copies, waits for them, and re-layouts, gathered(): whole = lax.dynamic_update_slice_in_dim(whole, piece, at, 0)  39.3 us
    dot_general x6, matrix products, mm_nt(): return jnp.einsum('ik,jk->ij', a, b, preferred_element_type=f32)  37.4 us
    dot_general x6, matrix products, mm(): return jnp.dot(a, b, preferred_element_type=f32)  29.7 us
    dot_general x6, matrix products, mm_tn(): return jnp.einsum('ki,kj->ij', a, b, preferred_element_type=f32)  28.9 us
  transfers between devices with their start and end apart: 94, of which 42 were waited for; matrix products, arithmetic and copies ran while one was open for 31% of the time, Pallas kernels for 0%

profile of v1, /device:TPU:6, one launch (start us, length us, event | category | flops | bytes accessed | tf_op | source)
XLA Modules:
  0.0 741.5 jit_solution(15915397586619491915)
XLA Ops:
  8.7 4.5 collective-permute-start.28
  13.2 7.6 %collective-permute-done.28 = bf16[70,1536]{1,0:T(8,128)(2,1)S(1)} collective-permute-done((bf16[70,1536]{1,0:T(8,128)(2,1)S(1)}, bf16[70,1536]{1,0:T(8,128)(2,1)S(1)}, u32[]{:S(2)}, u32[]{:S(2)}) %collective-permute-start.28) | collective-permute-done | bytes 215072 | tf_op jit(solution)/shard_map/ppermute | solution.py:217
  29.3 9.8 %collective-permute-start.11 = (bf16[96,2176]{1,0:T(8,128)(2,1)S(1)}, bf16[96,2176]{1,0:T(8,128)(2,1)S(1)}, u32[]{:S(2)}, u32[]{:S(2)}) collective-permute-start(bf16[96,2176]{1,0:T(8,128)(2,1)S(1)} %pad_dynamic-update-slice_fusion), channel_id=1, source_target_pairs={{0,6},{2,0},{4,2},{6,4},{1,7},{3,1},{5,3},{7,5},{8,14},{10,8},{12,... | collective-permute-start | bytes 1253384 | tf_op jit(solution)/shard_map/ppermute | solution.py:30
  59.2 6.8 collective-permute-start.31
  72.1 6.9 collective-permute-start.2
  86.7 8.1 %collective-permute-done.12 = bf16[96,2176]{1,0:T(8,128)(2,1)S(1)} collective-permute-done((bf16[96,2176]{1,0:T(8,128)(2,1)}, bf16[96,2176]{1,0:T(8,128)(2,1)S(1)}, u32[]{:S(2)}, u32[]{:S(2)}) %collective-permute-start.12) | collective-permute-done | bytes 417824 | tf_op jit(solution)/shard_map/ppermute | solution.py:30
  99.3 11.5 %collective-permute-done.14 = bf16[48,2176]{1,0:T(8,128)(2,1)S(1)} collective-permute-done((bf16[48,2176]{1,0:T(8,128)(2,1)S(1)}, bf16[48,2176]{1,0:T(8,128)(2,1)S(1)}, u32[]{:S(2)}, u32[]{:S(2)}) %collective-permute-start.14) | collective-permute-done | bytes 208928 | tf_op jit(solution)/shard_map/ppermute | solution.py:30
  111.4 5.1 collective-permute-done.15
  118.6 9.5 %collective-permute-done.16 = bf16[48,2176]{1,0:T(8,128)(2,1)S(1)} collective-permute-done((bf16[48,2176]{1,0:T(8,128)(2,1)S(1)}, bf16[48,2176]{1,0:T(8,128)(2,1)S(1)}, u32[]{:S(2)}, u32[]{:S(2)}) %collective-permute-start.16) | collective-permute-done | bytes 208928 | tf_op jit(solution)/shard_map/ppermute | solution.py:29
  130.4 9.5 %collective-permute-done.17 = bf16[48,2176]{1,0:T(8,128)(2,1)S(1)} collective-permute-done((bf16[48,2176]{1,0:T(8,128)(2,1)S(1)}, bf16[48,2176]{1,0:T(8,128)(2,1)S(1)}, u32[]{:S(2)}, u32[]{:S(2)}) %collective-permute-start.17) | collective-permute-done | bytes 208928 | tf_op jit(solution)/shard_map/ppermute | solution.py:29
  142.3 9.8 %collective-permute-done.32 = bf16[128,1536]{1,0:T(8,128)(2,1)S(1)} collective-permute-done((bf16[128,1536]{1,0:T(8,128)(2,1)}, bf16[128,1536]{1,0:T(8,128)(2,1)S(1)}, u32[]{:S(2)}, u32[]{:S(2)}) %collective-permute-start.32) | collective-permute-done | bytes 393248 | tf_op jit(solution)/shard_map/ppermute | solution.py:30
  152.9 4.7 collective-permute-done.3
  166.4 6.3 collective-permute-done.6
  191.7 4.3 fusion.25
  206.2 13.0 %all_to_all.25 = bf16[8,192,128]{2,1,0:T(8,128)(2,1)S(1)} all-to-all(bf16[8,192,128]{2,1,0:T(8,128)(2,1)S(1)} %pad_maximum_fusion.8), channel_id=1, replica_groups=mesh['y'=4,'xl'=2,'xh'=2,'z'=4,'core'=2] {'y','xl'}, dimensions={0} | all-to-all | bytes 786432 | tf_op jit(solution)/shard_map/all_to_all | solution.py:267
  230.1 6.2 collective-permute-done.20
  253.8 4.7 reshape.468
  258.5 10.6 %fusion.140 = f32[1024,2304]{1,0:T(8,128)S(1)} fusion(bf16[1024,1536]{1,0:T(8,128)(2,1)} %constant_dynamic-update-slice_fusion.30, bf16[1536,2304]{1,0:T(8,128)(2,1)} %all-gather.7.cloned.1.call-done), kind=kOutput, calls=%fused_computation.367 | convolution fusion | flops 7247757312 | bytes 19660800 | tf_op jit(solution)/shard_map/dot_general | solution.py:154
  269.1 10.2 %multiply_convert_fusion.1 = (bf16[1024,1120]{1,0:T(8,128)(2,1)}, bf16[1024,1120]{1,0:T(8,128)(2,1)}, bf16[1024,1120]{1,0:T(8,128)(2,1)S(1)}) fusion(f32[1024,2304]{1,0:T(8,128)S(1)} %fusion.140, bf16[1024,1536]{1,0:T(8,128)(2,1)} %get-tuple-element.122, bf16[1120,1536]{1,0:T(8,128)(2,1)S(1)} %copy-done.11), kind=kOutput, calls=%fused_computation.21 | convolution fusion | flops 3540418560 | bytes 22642688 | tf_op jit(solution)/shard_map/ik,jk->ij/dot_general | solution.py:158
  280.7 7.5 %convolution_convert_fusion.1 = bf16[1120,1536]{1,0:T(8,128)(2,1)} fusion(bf16[1024,1120]{1,0:T(8,128)(2,1)S(1)} %get-tuple-element.25, bf16[1024,1536]{1,0:T(8,128)(2,1)} %get-tuple-element.122), kind=kOutput, calls=%fused_computation.3 | convolution fusion | flops 3524935680 | bytes 8880128 | tf_op jit(solution)/shard_map/ki,kj->ij/dot_general | solution.py:162
  288.1 42.1 %fusion = bf16[72,1536]{1,0:T(8,128)(2,1)S(1)} fusion(bf16[1120,1536]{1,0:T(8,128)(2,1)} %convolution_convert_fusion.1), kind=kCustom, calls=%all-reduce-scatter | all-reduce-scatter fusion | flops 1769473 | bytes 3662336
  333.4 6.4 collective-permute-done.84
  342.2 11.1 %collective-permute-done.83 = bf16[70,1536]{1,0:T(8,128)(2,1)S(1)} collective-permute-done((bf16[70,1536]{1,0:T(8,128)(2,1)S(1)}, bf16[70,1536]{1,0:T(8,128)(2,1)S(1)}, u32[]{:S(2)}, u32[]{:S(2)}) %collective-permute-start.83) | collective-permute-done | bytes 215072 | tf_op jit(solution)/shard_map/ppermute | solution.py:369
  354.1 8.5 %convolution_convert_fusion.4 = bf16[1024,1536]{1,0:T(8,128)(2,1)} fusion(bf16[1024,1120]{1,0:T(8,128)(2,1)} %copy-done.47, bf16[1120,1536]{1,0:T(8,128)(2,1)} %reshape.468), kind=kOutput, calls=%fused_computation.31 | convolution fusion | flops 3524788224 | bytes 8880128 | tf_op jit(solution)/shard_map/dot_general | solution.py:154
  362.7 8.2 %concatenate.139 = bf16[1024,2304]{1,0:T(8,128)(2,1)} concatenate(bf16[1024,1120]{1,0:T(8,128)(2,1)} %get-tuple-element.24, bf16[1024,32]{1,0:T(8,128)(2,1)S(1)} %broadcast_in_dim.88, bf16[1024,1120]{1,0:T(8,128)(2,1)} %get-tuple-element.23, bf16[1024,32]{1,0:T(8,128)(2,1)S(1)} %broadcast_in_dim.88), dimensions={1} | concatenate | bytes 9437184 | tf_op jit(solution)/shard_map/concatenate | solution.py:286
  370.9 10.6 %convolution_convert_fusion = bf16[1536,2304]{1,0:T(8,128)(2,1)S(1)} fusion(bf16[1024,1536]{1,0:T(8,128)(2,1)} %constant_dynamic-update-slice_fusion.30, bf16[1024,2304]{1,0:T(8,128)(2,1)} %concatenate.139), kind=kOutput, calls=%fused_computation | convolution fusion | flops 7251296256 | bytes 14942208 | tf_op jit(solution)/shard_map/ki,kj->ij/dot_general | solution.py:162
  385.7 6.4 collective-permute-done.65
  392.0 3.9 fusion.1
  397.1 11.3 %convolution_convert_fusion.3 = bf16[1024,1536]{1,0:T(8,128)(2,1)} fusion(bf16[1024,2304]{1,0:T(8,128)(2,1)S(1)} %bitcast.319, bf16[1536,2304]{1,0:T(8,128)(2,1)} %all-gather.7.cloned.1.call-done), kind=kOutput, calls=%fused_computation.30 | convolution fusion | flops 7249330176 | bytes 14942208 | tf_op jit(solution)/shard_map/ik,jk->ij/dot_general | solution.py:158
  408.5 7.2 all-to-all-start.1
  424.1 6.1 collective-permute-done.67
  446.3 56.2 %collective-permute-done.68 = bf16[96,2304]{1,0:T(8,128)(2,1)S(1)} collective-permute-done((bf16[96,2304]{1,0:T(8,128)(2,1)}, bf16[96,2304]{1,0:T(8,128)(2,1)S(1)}, u32[]{:S(2)}, u32[]{:S(2)}) %collective-permute-start.68) | collective-permute-done | bytes 442400 | tf_op jit(solution)/shard_map/ppermute | solution.py:29
  545.5 3.7 slice_bitcast_fusion.2
  549.2 8.3 %concatenate.164 = bf16[96,17920]{1,0:T(8,128)(2,1)} concatenate(bf16[96,1120]{1,0:T(8,128)(2,1)} %get-tuple-element.45, bf16[96,1120]{1,0:T(8,128)(2,1)} %get-tuple-element.44, bf16[96,1120]{1,0:T(8,128)(2,1)} %get-tuple-element.43, bf16[96,1120]{1,0:T(8,128)(2,1)} %get-tuple-element.42, bf16[96,1120]{1,0:T(8,128)(2,1)} %get-tuple-element.41, ...), dimensions={1} | concatenate | bytes 6881280 | tf_op jit(solution)/shard_map/concatenate | solution.py:373
  557.5 7.0 multiply_reduce_fusion
  567.4 4.0 fusion.16
  573.5 4.5 all-to-all-start.2
  583.1 5.0 all-to-all-done.2
  588.2 4.6 multiply_reduce_fusion.1
  599.1 4.2 fusion.28
  604.7 6.4 all-to-all-start.3
  616.4 4.1 convolution_convert_fusion.5
  626.7 6.0 fusion.42
  651.5 4.4 collective-permute-start.49
  657.2 6.1 collective-permute-start.48
  670.8 6.2 collective-permute-done.54
  688.1 5.7 all-to-all-start.4
  694.9 5.9 all-to-all-done.4
  (513 shorter events, 303.9 us)
Async XLA Ops:
  7.2 246.6 %all-gather.11.cloned.1.call-start = ((), (), s32[]{:S(2)}) async-start(), calls=%async_computation.9 | async-start | bytes 3760128 | tf_op jit(solution)/shard_map/all_gather | solution.py:218
  21.5 237.0 %all-gather.7.cloned.1.call-start = ((), (), s32[]{:S(2)}) async-start(), calls=%async_computation.6 | async-start | bytes 7520256 | tf_op jit(solution)/shard_map/all_gather | solution.py:212
  27.8 52.1 %collective-permute-start.9 = (bf16[96,2176]{1,0:T(8,128)(2,1)S(1)}, bf16[96,2176]{1,0:T(8,128)(2,1)}, u32[]{:S(2)}, u32[]{:S(2)}) collective-permute-start(bf16[96,2176]{1,0:T(8,128)(2,1)S(1)} %pad_dynamic-update-slice_fusion), channel_id=1, source_target_pairs={{0,8},{8,0},{1,9},{9,1},{2,10},{10,2},{3,11},{11,3},{4,12},{12,4},... | collective-permute-start | bytes 1253384 | tf_op jit(solution)/shard_map/ppermute | solution.py:29
  27.9 53.9 %collective-permute-start.10 = (bf16[96,2176]{1,0:T(8,128)(2,1)S(1)}, bf16[96,2176]{1,0:T(8,128)(2,1)S(1)}, u32[]{:S(2)}, u32[]{:S(2)}) collective-permute-start(bf16[96,2176]{1,0:T(8,128)(2,1)S(1)} %pad_dynamic-update-slice_fusion), channel_id=1, source_target_pairs={{0,2},{2,4},{4,6},{6,0},{1,3},{3,5},{5,7},{7,1},{8,10},{10,12},{12... | collective-permute-start | bytes 1253384 | tf_op jit(solution)/shard_map/ppermute | solution.py:30
  29.3 55.5 %collective-permute-start.11 = (bf16[96,2176]{1,0:T(8,128)(2,1)S(1)}, bf16[96,2176]{1,0:T(8,128)(2,1)S(1)}, u32[]{:S(2)}, u32[]{:S(2)}) collective-permute-start(bf16[96,2176]{1,0:T(8,128)(2,1)S(1)} %pad_dynamic-update-slice_fusion), channel_id=1, source_target_pairs={{0,6},{2,0},{4,2},{6,4},{1,7},{3,1},{5,3},{7,5},{8,14},{10,8},{12,... | collective-permute-start | bytes 1253384 | tf_op jit(solution)/shard_map/ppermute | solution.py:30
  39.1 13.1 %collective-permute-start.29 = (bf16[128,1536]{1,0:T(8,128)(2,1)}, bf16[128,1536]{1,0:T(8,128)(2,1)}, u32[]{:S(2)}, u32[]{:S(2)}) collective-permute-start(bf16[128,1536]{1,0:T(8,128)(2,1)} %bitcast.333), channel_id=1, source_target_pairs={{0,16},{16,0},{1,17},{17,1},{2,18},{18,2},{3,19},{19,3},{4,20},{20... | collective-permute-start | bytes 1179656 | tf_op jit(solution)/shard_map/ppermute | solution.py:29
  39.5 19.7 %collective-permute-start = (bf16[128,1536]{1,0:T(8,128)(2,1)}, bf16[128,1536]{1,0:T(8,128)(2,1)S(1)}, u32[]{:S(2)}, u32[]{:S(2)}) collective-permute-start(bf16[128,1536]{1,0:T(8,128)(2,1)} %bitcast.320), channel_id=1, source_target_pairs={{0,16},{16,0},{1,17},{17,1},{2,18},{18,2},{3,19},{19,3},{4,20},{20... | collective-permute-start | bytes 1179656 | tf_op jit(solution)/shard_map/ppermute | solution.py:29
  43.3 469.5 %all-gather.13.cloned.1.call-start = ((), (), s32[]{:S(2)}) async-start(), calls=%async_computation.10 | async-start | bytes 1990656 | tf_op jit(solution)/shard_map/all_gather | solution.py:370
  52.2 15.6 %collective-permute-start.30 = (bf16[128,1536]{1,0:T(8,128)(2,1)S(1)}, bf16[128,1536]{1,0:T(8,128)(2,1)S(1)}, u32[]{:S(2)}, u32[]{:S(2)}) collective-permute-start(bf16[128,1536]{1,0:T(8,128)(2,1)S(1)} %bitcast.334), channel_id=1, source_target_pairs={{0,32},{32,64},{64,96},{96,0},{1,33},{33,65},{65,97},{97,1},{2,34}... | collective-permute-start | bytes 1179656 | tf_op jit(solution)/shard_map/ppermute | solution.py:30
  59.2 12.9 %collective-permute-start.31 = (bf16[128,1536]{1,0:T(8,128)(2,1)S(1)}, bf16[128,1536]{1,0:T(8,128)(2,1)S(1)}, u32[]{:S(2)}, u32[]{:S(2)}) collective-permute-start(bf16[128,1536]{1,0:T(8,128)(2,1)S(1)} %bitcast.335), channel_id=1, source_target_pairs={{0,96},{32,0},{64,32},{96,64},{1,97},{33,1},{65,33},{97,65},{2,98}... | collective-permute-start | bytes 1179656 | tf_op jit(solution)/shard_map/ppermute | solution.py:30
  67.8 72.8 %collective-permute-start.1 = (bf16[128,1536]{1,0:T(8,128)(2,1)S(1)}, bf16[128,1536]{1,0:T(8,128)(2,1)S(1)}, u32[]{:S(2)}, u32[]{:S(2)}) collective-permute-start(bf16[128,1536]{1,0:T(8,128)(2,1)S(1)} %bitcast.321), channel_id=1, source_target_pairs={{0,32},{32,64},{64,96},{96,0},{1,33},{33,65},{65,97},{97,1},{2,34}... | collective-permute-start | bytes 1179656 | tf_op jit(solution)/shard_map/ppermute | solution.py:30
  72.1 69.2 %collective-permute-start.2 = (bf16[128,1536]{1,0:T(8,128)(2,1)S(1)}, bf16[128,1536]{1,0:T(8,128)(2,1)S(1)}, u32[]{:S(2)}, u32[]{:S(2)}) collective-permute-start(bf16[128,1536]{1,0:T(8,128)(2,1)S(1)} %bitcast.322), channel_id=1, source_target_pairs={{0,96},{32,0},{64,32},{96,64},{1,97},{33,1},{65,33},{97,65},{2,98}... | collective-permute-start | bytes 1179656 | tf_op jit(solution)/shard_map/ppermute | solution.py:30
  79.9 82.8 %collective-permute-start.34 = (bf16[64,1536]{1,0:T(8,128)(2,1)S(1)}, bf16[64,1536]{1,0:T(8,128)(2,1)S(1)}, u32[]{:S(2)}, u32[]{:S(2)}) collective-permute-start(bf16[64,1536]{1,0:T(8,128)(2,1)S(1)} %slice.479), channel_id=1, source_target_pairs={{0,32},{32,64},{64,96},{96,0},{1,33},{33,65},{65,97},{97,1},{2,34}... | collective-permute-start | bytes 589832 | tf_op jit(solution)/shard_map/ppermute | solution.py:30
  81.8 13.0 %collective-permute-start.12 = (bf16[96,2176]{1,0:T(8,128)(2,1)}, bf16[96,2176]{1,0:T(8,128)(2,1)S(1)}, u32[]{:S(2)}, u32[]{:S(2)}) collective-permute-start(bf16[96,2176]{1,0:T(8,128)(2,1)} %collective-permute-done.9), channel_id=1, source_target_pairs={{0,2},{2,4},{4,6},{6,0},{1,3},{3,5},{5,7},{7,1},{8,10},{10,12},{12... | collective-permute-start | bytes 1253384 | tf_op jit(solution)/shard_map/ppermute | solution.py:30
  84.8 13.7 %collective-permute-start.13 = (bf16[96,2176]{1,0:T(8,128)(2,1)}, bf16[96,2176]{1,0:T(8,128)(2,1)S(1)}, u32[]{:S(2)}, u32[]{:S(2)}) collective-permute-start(bf16[96,2176]{1,0:T(8,128)(2,1)} %collective-permute-done.9), channel_id=1, source_target_pairs={{0,6},{2,0},{4,2},{6,4},{1,7},{3,1},{5,3},{7,5},{8,14},{10,8},{12,... | collective-permute-start | bytes 1253384 | tf_op jit(solution)/shard_map/ppermute | solution.py:30
  94.8 68.6 %collective-permute-start.35 = (bf16[64,1536]{1,0:T(8,128)(2,1)S(1)}, bf16[64,1536]{1,0:T(8,128)(2,1)S(1)}, u32[]{:S(2)}, u32[]{:S(2)}) collective-permute-start(bf16[64,1536]{1,0:T(8,128)(2,1)S(1)} %slice.480), channel_id=1, source_target_pairs={{0,96},{32,0},{64,32},{96,64},{1,97},{33,1},{65,33},{97,65},{2,98}... | collective-permute-start | bytes 589832 | tf_op jit(solution)/shard_map/ppermute | solution.py:30
  98.5 12.3 %collective-permute-start.14 = (bf16[48,2176]{1,0:T(8,128)(2,1)S(1)}, bf16[48,2176]{1,0:T(8,128)(2,1)S(1)}, u32[]{:S(2)}, u32[]{:S(2)}) collective-permute-start(bf16[48,2176]{1,0:T(8,128)(2,1)S(1)} %slice.454), channel_id=1, source_target_pairs={{0,2},{2,4},{4,6},{6,0},{1,3},{3,5},{5,7},{7,1},{8,10},{10,12},{12... | collective-permute-start | bytes 626696 | tf_op jit(solution)/shard_map/ppermute | solution.py:30
  139.9 12.2 %collective-permute-start.32 = (bf16[128,1536]{1,0:T(8,128)(2,1)}, bf16[128,1536]{1,0:T(8,128)(2,1)S(1)}, u32[]{:S(2)}, u32[]{:S(2)}) collective-permute-start(bf16[128,1536]{1,0:T(8,128)(2,1)} %collective-permute-done.29), channel_id=1, source_target_pairs={{0,32},{32,64},{64,96},{96,0},{1,33},{33,65},{65,97},{97,1},{2,34}... | collective-permute-start | bytes 1179656 | tf_op jit(solution)/shard_map/ppermute | solution.py:30
  140.6 43.2 %collective-permute-start.18 = (bf16[768,2176]{1,0:T(8,128)(2,1)}, bf16[768,2176]{1,0:T(8,128)(2,1)S(1)}, u32[]{:S(2)}, u32[]{:S(2)}) collective-permute-start(bf16[768,2176]{1,0:T(8,128)(2,1)} %constant_dynamic-update-slice_fusion.40), channel_id=1, source_target_pairs={{0,1},{1,0},{2,3},{3,2},{4,5},{5,4},{6,7},{7,6},{8,9},{9,8},{10,11... | collective-permute-start | bytes 10027016 | tf_op jit(solution)/shard_map/ppermute | solution.py:110
  141.4 16.1 %collective-permute-start.3 = (bf16[128,1536]{1,0:T(8,128)(2,1)S(1)}, bf16[128,1536]{1,0:T(8,128)(2,1)S(1)}, u32[]{:S(2)}, u32[]{:S(2)}) collective-permute-start(bf16[128,1536]{1,0:T(8,128)(2,1)S(1)} %copy-done.24), channel_id=1, source_target_pairs={{0,32},{32,64},{64,96},{96,0},{1,33},{33,65},{65,97},{97,1},{2,34}... | collective-permute-start | bytes 1179656 | tf_op jit(solution)/shard_map/ppermute | solution.py:30
  161.9 12.4 %collective-permute-start.4 = (bf16[128,1536]{1,0:T(8,128)(2,1)S(1)}, bf16[128,1536]{1,0:T(8,128)(2,1)S(1)}, u32[]{:S(2)}, u32[]{:S(2)}) collective-permute-start(bf16[128,1536]{1,0:T(8,128)(2,1)S(1)} %copy-done.24), channel_id=1, source_target_pairs={{0,96},{32,0},{64,32},{96,64},{1,97},{33,1},{65,33},{97,65},{2,98}... | collective-permute-start | bytes 1179656 | tf_op jit(solution)/shard_map/ppermute | solution.py:30
  163.4 14.2 %collective-permute-start.36 = (bf16[64,1536]{1,0:T(8,128)(2,1)S(1)}, bf16[64,1536]{1,0:T(8,128)(2,1)S(1)}, u32[]{:S(2)}, u32[]{:S(2)}) collective-permute-start(bf16[64,1536]{1,0:T(8,128)(2,1)S(1)} %collective-permute-done.34), channel_id=1, source_target_pairs={{0,16},{16,0},{1,17},{17,1},{2,18},{18,2},{3,19},{19,3},{4,20},{20... | collective-permute-start | bytes 589832 | tf_op jit(solution)/shard_map/ppermute | solution.py:29
  165.1 14.0 %collective-permute-start.37 = (bf16[64,1536]{1,0:T(8,128)(2,1)S(1)}, bf16[64,1536]{1,0:T(8,128)(2,1)S(1)}, u32[]{:S(2)}, u32[]{:S(2)}) collective-permute-start(bf16[64,1536]{1,0:T(8,128)(2,1)S(1)} %collective-permute-done.35), channel_id=1, source_target_pairs={{0,16},{16,0},{1,17},{17,1},{2,18},{18,2},{3,19},{19,3},{4,20},{20... | collective-permute-start | bytes 589832 | tf_op jit(solution)/shard_map/ppermute | solution.py:29
  340.3 13.0 %collective-permute-start.83 = (bf16[70,1536]{1,0:T(8,128)(2,1)S(1)}, bf16[70,1536]{1,0:T(8,128)(2,1)S(1)}, u32[]{:S(2)}, u32[]{:S(2)}) collective-permute-start(bf16[70,1536]{1,0:T(8,128)(2,1)S(1)} %constant_dynamic-slice_fusion.11), channel_id=1, source_target_pairs={{0,0},{1,16},{2,32},{3,48},{4,64},{5,80},{6,96},{7,112},{8,1},{9,1... | collective-permute-start | bytes 645128 | tf_op jit(solution)/shard_map/ppermute | solution.py:369
  354.0 211.0 %reduce-scatter.4.cloned.1.call-start = ((), (), s32[]{:S(2)}) async-start(), calls=%async_computation.7 | async-start | bytes 3538944 | tf_op jit(solution)/shard_map/reduce_scatter | solution.py:291
  362.6 264.0 %all-gather.9.cloned.1.call-start = ((), (), s32[]{:S(2)}) async-start(), calls=%async_computation.8 | async-start | bytes 6684672 | tf_op jit(solution)/shard_map/all_gather | solution.py:219
  397.1 23.0 %collective-permute-start.69 = (bf16[96,2304]{1,0:T(8,128)(2,1)}, bf16[96,2304]{1,0:T(8,128)(2,1)S(1)}, u32[]{:S(2)}, u32[]{:S(2)}) collective-permute-start(bf16[96,2304]{1,0:T(8,128)(2,1)} %get-tuple-element.47), channel_id=1, source_target_pairs={{0,8},{8,0},{1,9},{9,1},{2,10},{10,2},{3,11},{11,3},{4,12},{12,4},... | collective-permute-start | bytes 1327112 | tf_op jit(solution)/shard_map/ppermute | solution.py:29
  408.5 101.8 %all-to-all-start.1 = ((bf16[8,128,1536]{2,1,0:T(8,128)(2,1)}), bf16[8,128,1536]{2,1,0:T(8,128)(2,1)}, u32[]{:S(2)}, u32[]{:S(2)}) async-start(bf16[8,128,1536]{2,1,0:T(8,128)(2,1)} %bitcast.323), calls=%async_computation.2 | async-start | bytes 6291456 | tf_op jit(solution)/shard_map/all_to_all | solution.py:137
  415.7 14.5 %collective-permute-start.67 = (bf16[96,2304]{1,0:T(8,128)(2,1)}, bf16[96,2304]{1,0:T(8,128)(2,1)S(1)}, u32[]{:S(2)}, u32[]{:S(2)}) collective-permute-start(bf16[96,2304]{1,0:T(8,128)(2,1)} %get-tuple-element.48), channel_id=1, source_target_pairs={{0,2},{2,4},{4,6},{6,0},{1,3},{3,5},{5,7},{7,1},{8,10},{10,12},{12... | collective-permute-start | bytes 1327112 | tf_op jit(solution)/shard_map/ppermute | solution.py:30
  419.1 13.3 %collective-permute-start.66 = (bf16[96,2304]{1,0:T(8,128)(2,1)}, bf16[96,2304]{1,0:T(8,128)(2,1)S(1)}, u32[]{:S(2)}, u32[]{:S(2)}) collective-permute-start(bf16[96,2304]{1,0:T(8,128)(2,1)} %get-tuple-element.46), channel_id=1, source_target_pairs={{0,6},{2,0},{4,2},{6,4},{1,7},{3,1},{5,3},{7,5},{8,14},{10,8},{12,... | collective-permute-start | bytes 1327112 | tf_op jit(solution)/shard_map/ppermute | solution.py:30
  421.3 16.3 %collective-permute-start.70 = (bf16[48,2304]{1,0:T(8,128)(2,1)S(1)}, bf16[48,2304]{1,0:T(8,128)(2,1)S(1)}, u32[]{:S(2)}, u32[]{:S(2)}) collective-permute-start(bf16[48,2304]{1,0:T(8,128)(2,1)S(1)} %get-tuple-element.28), channel_id=1, source_target_pairs={{0,6},{2,0},{4,2},{6,4},{1,7},{3,1},{5,3},{7,5},{8,14},{10,8},{12,... | collective-permute-start | bytes 663560 | tf_op jit(solution)/shard_map/ppermute | solution.py:30
  424.1 13.5 %collective-permute-start.72 = (bf16[48,2304]{1,0:T(8,128)(2,1)S(1)}, bf16[48,2304]{1,0:T(8,128)(2,1)S(1)}, u32[]{:S(2)}, u32[]{:S(2)}) collective-permute-start(bf16[48,2304]{1,0:T(8,128)(2,1)S(1)} %get-tuple-element.29), channel_id=1, source_target_pairs={{0,2},{2,4},{4,6},{6,0},{1,3},{3,5},{5,7},{7,1},{8,10},{10,12},{12... | collective-permute-start | bytes 663560 | tf_op jit(solution)/shard_map/ppermute | solution.py:30
  434.3 68.2 %collective-permute-start.68 = (bf16[96,2304]{1,0:T(8,128)(2,1)}, bf16[96,2304]{1,0:T(8,128)(2,1)S(1)}, u32[]{:S(2)}, u32[]{:S(2)}) collective-permute-start(bf16[96,2304]{1,0:T(8,128)(2,1)} %fusion.38), channel_id=1, source_target_pairs={{0,8},{8,0},{1,9},{9,1},{2,10},{10,2},{3,11},{11,3},{4,12},{12,4},... | collective-permute-start | bytes 1327112 | tf_op jit(solution)/shard_map/ppermute | solution.py:29
  439.6 62.9 %collective-permute-start.73 = (bf16[96,2304]{1,0:T(8,128)(2,1)}, bf16[96,2304]{1,0:T(8,128)(2,1)}, u32[]{:S(2)}, u32[]{:S(2)}) collective-permute-start(bf16[96,2304]{1,0:T(8,128)(2,1)} %pad_maximum_fusion.6), channel_id=1, source_target_pairs={{0,2},{2,4},{4,6},{6,0},{1,3},{3,5},{5,7},{7,1},{8,10},{10,12},{12... | collective-permute-start | bytes 1327112 | tf_op jit(solution)/shard_map/ppermute | solution.py:30
  442.5 60.1 %collective-permute-start.71 = (bf16[96,2304]{1,0:T(8,128)(2,1)}, bf16[96,2304]{1,0:T(8,128)(2,1)}, u32[]{:S(2)}, u32[]{:S(2)}) collective-permute-start(bf16[96,2304]{1,0:T(8,128)(2,1)} %pad_maximum_fusion.5), channel_id=1, source_target_pairs={{0,6},{2,0},{4,2},{6,4},{1,7},{3,1},{5,3},{7,5},{8,14},{10,8},{12,... | collective-permute-start | bytes 1327112 | tf_op jit(solution)/shard_map/ppermute | solution.py:30
  507.0 21.8 %collective-permute-start.74 = (bf16[96,2304]{1,0:T(8,128)(2,1)}, bf16[96,2304]{1,0:T(8,128)(2,1)}, u32[]{:S(2)}, u32[]{:S(2)}) collective-permute-start(bf16[96,2304]{1,0:T(8,128)(2,1)} %get-tuple-element.18), channel_id=1, source_target_pairs={{0,16},{16,0},{1,17},{17,1},{2,18},{18,2},{3,19},{19,3},{4,20},{20... | collective-permute-start | bytes 1327112 | tf_op jit(solution)/shard_map/ppermute | solution.py:29
  508.6 13.7 %collective-permute-start.76 = (bf16[96,2304]{1,0:T(8,128)(2,1)}, bf16[96,2304]{1,0:T(8,128)(2,1)}, u32[]{:S(2)}, u32[]{:S(2)}) collective-permute-start(bf16[96,2304]{1,0:T(8,128)(2,1)} %get-tuple-element.18), channel_id=1, source_target_pairs={{0,96},{32,0},{64,32},{96,64},{1,97},{33,1},{65,33},{97,65},{2,98}... | collective-permute-start | bytes 1327112 | tf_op jit(solution)/shard_map/ppermute | solution.py:30
  518.2 18.3 %collective-permute-start.79 = (bf16[48,2304]{1,0:T(8,128)(2,1)S(1)}, bf16[48,2304]{1,0:T(8,128)(2,1)S(1)}, u32[]{:S(2)}, u32[]{:S(2)}) collective-permute-start(bf16[48,2304]{1,0:T(8,128)(2,1)S(1)} %slice.512), channel_id=1, source_target_pairs={{0,32},{32,64},{64,96},{96,0},{1,33},{33,65},{65,97},{97,1},{2,34}... | collective-permute-start | bytes 663560 | tf_op jit(solution)/shard_map/ppermute | solution.py:30
  523.3 13.3 %collective-permute-start.80 = (bf16[48,2304]{1,0:T(8,128)(2,1)S(1)}, bf16[48,2304]{1,0:T(8,128)(2,1)S(1)}, u32[]{:S(2)}, u32[]{:S(2)}) collective-permute-start(bf16[48,2304]{1,0:T(8,128)(2,1)S(1)} %slice.513), channel_id=1, source_target_pairs={{0,96},{32,0},{64,32},{96,64},{1,97},{33,1},{65,33},{97,65},{2,98}... | collective-permute-start | bytes 663560 | tf_op jit(solution)/shard_map/ppermute | solution.py:30
  573.5 14.6 %all-to-all-start.2 = ((bf16[8,192,128]{2,1,0:T(8,128)(2,1)}), bf16[8,192,128]{2,1,0:T(8,128)(2,1)S(1)}, u32[]{:S(2)}, u32[]{:S(2)}) async-start(bf16[8,192,128]{2,1,0:T(8,128)(2,1)} %copy.220), calls=%async_computation.3 | async-start | bytes 786432 | tf_op jit(solution)/shard_map/all_to_all | solution.py:310
  583.1 61.7 %collective-permute-start.47 = (bf16[8,96,1536]{2,1,0:T(8,128)(2,1)}, bf16[8,96,1536]{2,1,0:T(8,128)(2,1)}, u32[]{:S(2)}, u32[]{:S(2)}) collective-permute-start(bf16[8,96,1536]{2,1,0:T(8,128)(2,1)} %dynamic-slice_bitcast_fusion.1), channel_id=1, source_target_pairs={{0,1},{1,0},{2,3},{3,2},{4,5},{5,4},{6,7},{7,6},{8,9},{9,8},{10,11... | collective-permute-start | bytes 7077896 | tf_op jit(solution)/shard_map/ppermute | solution.py:110
  604.7 17.1 %all-to-all-start.3 = ((bf16[8,448,128]{2,1,0:T(8,128)(2,1)}), bf16[8,448,128]{2,1,0:T(8,128)(2,1)S(1)}, u32[]{:S(2)}, u32[]{:S(2)}) async-start(bf16[8,448,128]{2,1,0:T(8,128)(2,1)} %pad_maximum_fusion.1), calls=%async_computation.4 | async-start | bytes 1835008 | tf_op jit(solution)/shard_map/all_to_all | solution.py:337
  641.4 36.2 %collective-permute-start.43 = (bf16[56,512]{1,0:T(8,128)(2,1)S(1)}, bf16[56,512]{1,0:T(8,128)(2,1)S(1)}, u32[]{:S(2)}, u32[]{:S(2)}) collective-permute-start(bf16[56,512]{1,0:T(8,128)(2,1)S(1)} %get-tuple-element.76), channel_id=1, source_target_pairs={{0,6},{2,0},{4,2},{6,4},{1,7},{3,1},{5,3},{7,5},{8,14},{10,8},{12,... | collective-permute-start | bytes 172040 | tf_op jit(solution)/shard_map/ppermute | solution.py:30
  644.8 35.8 %collective-permute-start.45 = (bf16[56,512]{1,0:T(8,128)(2,1)S(1)}, bf16[56,512]{1,0:T(8,128)(2,1)S(1)}, u32[]{:S(2)}, u32[]{:S(2)}) collective-permute-start(bf16[56,512]{1,0:T(8,128)(2,1)S(1)} %get-tuple-element.77), channel_id=1, source_target_pairs={{0,2},{2,4},{4,6},{6,0},{1,3},{3,5},{5,7},{7,1},{8,10},{10,12},{12... | collective-permute-start | bytes 172040 | tf_op jit(solution)/shard_map/ppermute | solution.py:30
  649.5 44.4 %collective-permute-start.41 = (bf16[112,512]{1,0:T(8,128)(2,1)}, bf16[112,512]{1,0:T(8,128)(2,1)}, u32[]{:S(2)}, u32[]{:S(2)}) collective-permute-start(bf16[112,512]{1,0:T(8,128)(2,1)} %fusion.106), channel_id=1, source_target_pairs={{0,8},{8,0},{1,9},{9,1},{2,10},{10,2},{3,11},{11,3},{4,12},{12,4},... | collective-permute-start | bytes 344072 | tf_op jit(solution)/shard_map/ppermute | solution.py:29
  680.6 13.3 %collective-permute-start.46 = (bf16[112,512]{1,0:T(8,128)(2,1)S(1)}, bf16[112,512]{1,0:T(8,128)(2,1)}, u32[]{:S(2)}, u32[]{:S(2)}) collective-permute-start(bf16[112,512]{1,0:T(8,128)(2,1)S(1)} %pad_maximum_fusion.21), channel_id=1, source_target_pairs={{0,2},{2,4},{4,6},{6,0},{1,3},{3,5},{5,7},{7,1},{8,10},{10,12},{12... | collective-permute-start | bytes 344072 | tf_op jit(solution)/shard_map/ppermute | solution.py:30
  680.7 13.2 %collective-permute-start.44 = (bf16[112,512]{1,0:T(8,128)(2,1)S(1)}, bf16[112,512]{1,0:T(8,128)(2,1)}, u32[]{:S(2)}, u32[]{:S(2)}) collective-permute-start(bf16[112,512]{1,0:T(8,128)(2,1)S(1)} %pad_maximum_fusion.20), channel_id=1, source_target_pairs={{0,6},{2,0},{4,2},{6,4},{1,7},{3,1},{5,3},{7,5},{8,14},{10,8},{12,... | collective-permute-start | bytes 344072 | tf_op jit(solution)/shard_map/ppermute | solution.py:30
  688.1 12.7 %all-to-all-start.4 = ((bf16[8,96,192]{2,1,0:T(8,128)(2,1)}), bf16[8,96,192]{2,1,0:T(8,128)(2,1)S(1)}, u32[]{:S(2)}, u32[]{:S(2)}) async-start(bf16[8,96,192]{2,1,0:T(8,128)(2,1)} %copy.236), calls=%async_computation.5 | async-start | bytes 786432 | tf_op jit(solution)/shard_map/all_to_all | solution.py:362
  (100 other events, 1577.8 us)
Sparse Core Ops, SparseCore 0:
  21.6 60.6 all-gather.10
  85.4 71.2 all-gather.6
  354.1 47.3 all-gather.12
  403.8 127.2 reduce-scatter.3
  533.5 70.3 all-gather.8
